TPU v7x, 256 devices: a whole 4x4x8 slice. The times are simulated.
256 devices in a mesh: head: 8 (over x, y_hi), ctx: 32 (over z, y_lo, core).
Axes of the slice: x: 4, y: 4 (y_hi: 2, y_lo: 2; y = y_hi * 2 + y_lo), z: 8, core: 2. Of those that a mesh axis runs over, the one named last changes fastest.
Arguments:
- queries: bfloat16 [8192, 1024], P('ctx', 'head'), may hold values from -6 to 6
- keys: bfloat16 [8192, 1024], P('ctx', 'head'), may hold values from -6 to 6
- values: bfloat16 [8192, 1024], P('ctx', 'head'), may hold values from -6 to 6
- teacher_rows: bfloat16 [12288, 1024], P(('head', 'ctx')), may hold values from -3 to 3
- slots: int32 [12288], P(('head', 'ctx')), may hold values from 0 to 95, as said below
- spans: int32 [12288, 2], P(('head', 'ctx')), may hold values from 0 to 256, as said below
Outputs:
- grad_queries: bfloat16 [8192, 1024], P('ctx', 'head')
- grad_keys: bfloat16 [8192, 1024], P('ctx', 'head')
- grad_values: bfloat16 [8192, 1024], P('ctx', 'head')
Inputs may be any that keep to these rules, and one draw needn't show every extreme that they name: `slots`: in each block of 48 rows (the rows of one device) the values are distinct, so no block has more than 3 rows whose value // 3 is the same; in every draw one index of ctx gets exactly 3 rows from every block. `spans`: each span lies within the 256 student tokens of its index of ctx and covers 1 to 8 of them; some span covers exactly 8 and some ends at 256.
All inputs are finite; a program needn't handle non-finite values.
Results may differ from a plain program's by a relative error of at most 0.0076.
Values may be sent and summed in bfloat16 or wider, within the bound.
A program may use at most 64 MiB of HBM per device.

v0:
```python
import math

import jax
import jax.numpy as jnp
from jax import lax
from jax.sharding import PartitionSpec as P

DH = 128


masked_value = -1e30


def from_behind(x, axis, by):
    devices = lax.axis_size(axis)
    pairs = [(i, i + by) for i in range(devices) if 0 <= i + by < devices]
    return lax.ppermute(x, axis, pairs)


def from_behind_2(x, axis, by):
    devices = lax.axis_size(axis)
    return lax.ppermute(x, axis, [(i, (i + by) % devices) for i in range(devices)])


def block_scores(query_heads, key_heads, query_start, key_start, score_scale):
    query_pos = query_start + jnp.arange(query_heads.shape[0], dtype=jnp.int32)
    key_pos = key_start + jnp.arange(key_heads.shape[0], dtype=jnp.int32)
    visible = (key_pos[None, :] <= query_pos[:, None])[None]
    scores = (
        jnp.einsum("qhd,khd->hqk", query_heads, key_heads, preferred_element_type=jnp.float32)
        * score_scale
    )
    return (jnp.where(visible, scores, masked_value), visible)


def stats_visit(
    query_heads, grad_heads, key_heads, value_heads, query_start, key_start, stats, score_scale
):
    row_top, row_total, row_weighted = stats
    scores, visible = block_scores(query_heads, key_heads, query_start, key_start, score_scale)
    new_top = jnp.maximum(row_top, jnp.max(scores, axis=2))
    weights = jnp.where(visible, jnp.exp(scores - new_top[..., None]), 0.0)
    grad_prob = jnp.einsum(
        "qhd,khd->hqk", grad_heads, value_heads, preferred_element_type=jnp.float32
    )
    fade_out = jnp.exp(row_top - new_top)
    new_total = row_total * fade_out + jnp.sum(weights, axis=2)
    new_weighted = row_weighted * fade_out + jnp.sum(weights * grad_prob, axis=2)
    return (new_top, new_total, new_weighted)


def block_terms(
    query_heads,
    grad_heads,
    row_lse,
    row_delta,
    key_heads,
    value_heads,
    query_start,
    key_start,
    score_scale,
):
    scores, visible = block_scores(query_heads, key_heads, query_start, key_start, score_scale)
    prob = jnp.where(visible, jnp.exp(scores - row_lse[..., None]), 0.0)
    grad_prob = jnp.einsum(
        "qhd,khd->hqk", grad_heads, value_heads, preferred_element_type=jnp.float32
    )
    dscore = (prob * (grad_prob - row_delta[..., None]) * score_scale).astype(jnp.bfloat16)
    prob_half = prob.astype(jnp.bfloat16)
    grad_query = jnp.einsum("hqk,khd->qhd", dscore, key_heads, preferred_element_type=jnp.float32)
    grad_key = jnp.einsum("hqk,qhd->khd", dscore, query_heads, preferred_element_type=jnp.float32)
    grad_value = jnp.einsum(
        "hqk,qhd->khd", prob_half, grad_heads, preferred_element_type=jnp.float32
    )
    return (grad_query, grad_key, grad_value)


def stat_pass(key_block, value_block):
    return from_behind((key_block, value_block), "ctx", 1)


def grad_pass(key_sum, value_sum):
    return from_behind_2((key_sum, value_sum), "ctx", 1)


def shards(queries, keys, values, teacher_rows, slots, spans):
    cycle_size = lax.axis_size("ctx")
    position = lax.axis_index("ctx")
    head_count = lax.axis_size("head")
    row_count = queries.shape[0]
    local_heads = queries.shape[1] // DH
    score_scale = 1.0 / math.sqrt(DH)
    my_start = position * row_count
    capacity = 2 * teacher_rows.shape[0] // cycle_size
    row_width = teacher_rows.shape[1]
    packed = jnp.zeros((cycle_size * capacity, row_width), jnp.bfloat16).at[slots].set(teacher_rows)
    bounds = jnp.zeros((cycle_size * capacity, 2), jnp.int32).at[slots].set(spans)
    packed = packed.reshape(cycle_size, capacity, row_width)
    bounds = jnp.tile(bounds.reshape(cycle_size, capacity, 2), (1, 1, head_count))
    arrived, arrived_bounds = (
        lax.all_to_all(
            lax.all_to_all(packed, "head", split_axis=2, concat_axis=1, tiled=True),
            "ctx",
            split_axis=0,
            concat_axis=0,
            tiled=True,
        ),
        lax.all_to_all(
            lax.all_to_all(bounds, "head", split_axis=2, concat_axis=1, tiled=True),
            "ctx",
            split_axis=0,
            concat_axis=0,
            tiled=True,
        ),
    )
    arrived = arrived.reshape(-1, arrived.shape[2])
    arrived_bounds = arrived_bounds.reshape(-1, 2)
    token_pos = jnp.arange(row_count, dtype=jnp.int32)[:, None]
    coverage = (
        (token_pos >= arrived_bounds[None, :, 0]) & (token_pos < arrived_bounds[None, :, 1])
    ).astype(jnp.bfloat16)
    grad_rows = jnp.dot(coverage, arrived, preferred_element_type=jnp.float32).astype(jnp.bfloat16)
    query_heads = queries.reshape(row_count, local_heads, DH)
    key_heads = keys.reshape(row_count, local_heads, DH)
    value_heads = values.reshape(row_count, local_heads, DH)
    grad_heads = grad_rows.reshape(row_count, local_heads, DH)
    zero_stats = jnp.zeros((local_heads, row_count), jnp.float32)
    init_stats = (
        jnp.full((local_heads, row_count), masked_value, jnp.float32),
        zero_stats,
        zero_stats,
    )

    def stats_update(step, key_block, value_block, stats):
        source = (position - step) % cycle_size

        def visit(state):
            return stats_visit(
                query_heads,
                grad_heads,
                key_block,
                value_block,
                my_start,
                source * row_count,
                state,
                score_scale,
            )

        return lax.cond(source <= position, visit, lambda state: state, stats)

    def stats_loop(step, running):
        key_block, value_block, stats = running
        stats = stats_update(step, key_block, value_block, stats)
        key_block, value_block = stat_pass(key_block, value_block)
        return (key_block, value_block, stats)

    key_block, value_block, stats = lax.fori_loop(
        0, cycle_size - 1, stats_loop, (key_heads, value_heads, init_stats)
    )
    stats = stats_update(cycle_size - 1, key_block, value_block, stats)
    row_lse = stats[0] + jnp.log(stats[1])
    row_delta = stats[2] / stats[1]
    zero_heads = jnp.zeros((row_count, local_heads, DH), jnp.float32)

    def key_update(step, key_block, value_block, sums):
        source = (position - step) % cycle_size

        def visit(state):
            term_query, term_key, term_value = block_terms(
                query_heads,
                grad_heads,
                row_lse,
                row_delta,
                key_block,
                value_block,
                my_start,
                source * row_count,
                score_scale,
            )
            return (state[0] + term_query, state[1] + term_key, state[2] + term_value)

        return lax.cond(source <= position, visit, lambda state: state, sums)

    start_sums = (zero_heads, zero_heads, zero_heads)

    def key_loop(step, running):
        key_block, value_block, sums = running
        sums = key_update(step, key_block, value_block, sums)
        key_block, value_block = from_behind((key_block, value_block), "ctx", 1)
        key_sum, value_sum = grad_pass(sums[1], sums[2])
        return (key_block, value_block, (sums[0], key_sum, value_sum))

    key_block, value_block, sums = lax.fori_loop(
        0, cycle_size - 1, key_loop, (key_heads, value_heads, start_sums)
    )
    sums = key_update(cycle_size - 1, key_block, value_block, sums)
    key_sum, value_sum = (
        from_behind_2(sums[1].astype(jnp.bfloat16), "ctx", 1).astype(jnp.float32),
        from_behind_2(sums[2].astype(jnp.bfloat16), "ctx", 1).astype(jnp.float32),
    )
    query_sum = sums[0]
    out_width = local_heads * DH
    return (
        query_sum.reshape(row_count, out_width).astype(jnp.bfloat16),
        key_sum.reshape(row_count, out_width).astype(jnp.bfloat16),
        value_sum.reshape(row_count, out_width).astype(jnp.bfloat16),
    )


def solution(mesh):
    return jax.shard_map(
        shards,
        mesh=mesh,
        in_specs=(
            P("ctx", "head"),
            P("ctx", "head"),
            P("ctx", "head"),
            P(("head", "ctx"), None),
            P(("head", "ctx")),
            P(("head", "ctx"), None),
        ),
        out_specs=(P("ctx", "head"), P("ctx", "head"), P("ctx", "head")),
        check_vma=False,
    )
```

profile of v0, /device:TPU:37, one launch (start us, length us, event | category | flops | bytes accessed | tf_op | source)
XLA Modules:
  0.0 731.2 jit_solution(5208072516573428255)
XLA Ops:
  4.7 6.9 all-to-all-start
  16.0 5.7 all-to-all-start.2
  27.0 11.4 %all-to-all-start.1 = ((s32[32,24,2]{1,2,0:T(2,128)}), s32[32,24,2]{1,2,0:T(2,128)S(1)}, u32[]{:S(2)}, u32[]{:S(2)}) async-start(s32[32,24,2]{1,2,0:T(2,128)} %copy.45), calls=%async_computation.1 | async-start | bytes 65536 | tf_op jit(solution)/shard_map/all_to_all | solution.py:108
  40.3 5.1 all-to-all-done.1
  45.4 5.0 all-to-all-start.3
  50.6 9.4 %all-to-all-done.3 = bf16[32,24,128]{2,1,0:T(8,128)(2,1)S(1)} async-done(((bf16[32,24,128]{2,1,0:T(8,128)(2,1)}), bf16[32,24,128]{2,1,0:T(8,128)(2,1)S(1)}, u32[]{:S(2)}, u32[]{:S(2)}) %all-to-all-start.3) | async-done | bytes 196640 | tf_op jit(solution)/shard_map/all_to_all | solution.py:101
  60.9 324.6 %while.46 = (s32[]{:T(128)}, bf16[256,1,128]{2,0,1:T(8,128)(2,1)S(1)}, bf16[256,1,128]{2,0,1:T(8,128)(2,1)S(1)}, f32[1,256]{1,0:T(1,128)S(1)}, f32[1,256]{1,0:T(...) while((s32[]{:T(128)}, ...), condition=%wide.region_8.9_spmd, body=%wide.region_2.8_spmd.sunk | while | flops 34407696 | bytes 1862128 | solution.py:157
  99.2 4.3 collective-permute-start
  109.0 4.3 collective-permute-start
  118.9 4.3 collective-permute-start
  128.0 5.0 collective-permute-start
  157.3 5.0 collective-permute-start
  167.7 4.5 collective-permute-start
  178.8 4.5 collective-permute-start
  189.1 5.2 collective-permute-start
  200.1 4.5 collective-permute-start
  211.2 4.5 collective-permute-start
  221.5 4.7 collective-permute-start
  232.6 4.5 collective-permute-start
  243.7 4.5 collective-permute-start
  254.0 4.5 collective-permute-start
  265.1 4.5 collective-permute-start
  276.1 4.5 collective-permute-start
  286.5 4.5 collective-permute-start
  297.5 4.5 collective-permute-start
  308.6 4.5 collective-permute-start
  319.7 4.5 collective-permute-start
  330.7 4.5 collective-permute-start
  341.8 4.5 collective-permute-start
  352.9 4.5 collective-permute-start
  364.0 4.5 collective-permute-start
  375.0 4.5 collective-permute-start
  385.5 339.4 %while.47 = (s32[]{:T(128)}, bf16[256,1,128]{2,0,1:T(8,128)(2,1)S(1)}, bf16[256,1,128]{2,0,1:T(8,128)(2,1)S(1)}, f32[256,1,128]{2,0,1:T(8,128)S(1)}, f32[256,1,1...) while((s32[]{:T(128)}, ...), condition=%wide.region_17.18_spmd, body=%wide.region_14.17_spmd.sunk | while | flops 84640272 | bytes 4790880 | solution.py:193
  391.2 5.0 collective-permute-start.2
  406.3 5.2 collective-permute-start.2
  421.4 5.4 collective-permute-start.2
  434.7 5.2 collective-permute-start.2
  446.9 5.1 collective-permute-start.2
  479.9 5.1 collective-permute-start.2
  490.8 5.1 collective-permute-start.2
  511.7 5.1 collective-permute-start.2
  522.6 5.1 collective-permute-start.2
  543.5 5.1 collective-permute-start.2
  554.4 5.1 collective-permute-start.2
  575.3 5.1 collective-permute-start.2
  586.2 5.1 collective-permute-start.2
  607.0 5.1 collective-permute-start.2
  618.0 5.1 collective-permute-start.2
  (718 shorter events, 511.8 us)
Async XLA Ops:
  4.7 11.4 %all-to-all-start = ((s32[8,1,192]{2,1,0:T(1,128)}), s32[8,1,192]{2,1,0:T(1,128)S(1)}, u32[]{:S(2)}, u32[]{:S(2)}) async-start(s32[8,1,192]{2,1,0:T(1,128)} %reshape.263), calls=%async_computation | async-start | bytes 16384 | tf_op jit(solution)/shard_map/all_to_all | solution.py:109
  16.0 11.0 %all-to-all-start.2 = ((bf16[8,2,6144]{2,1,0:T(2,128)(2,1)}), bf16[8,2,6144]{2,1,0:T(2,128)(2,1)S(1)}, u32[]{:S(2)}, u32[]{:S(2)}) async-start(bf16[8,2,6144]{2,1,0:T(2,128)(2,1)} %reshape.261), calls=%async_computation.2 | async-start | bytes 393216 | tf_op jit(solution)/shard_map/all_to_all | solution.py:102
  27.0 18.4 %all-to-all-start.1 = ((s32[32,24,2]{1,2,0:T(2,128)}), s32[32,24,2]{1,2,0:T(2,128)S(1)}, u32[]{:S(2)}, u32[]{:S(2)}) async-start(s32[32,24,2]{1,2,0:T(2,128)} %copy.45), calls=%async_computation.1 | async-start | bytes 65536 | tf_op jit(solution)/shard_map/all_to_all | solution.py:108
  45.4 14.6 %all-to-all-start.3 = ((bf16[32,24,128]{2,1,0:T(8,128)(2,1)}), bf16[32,24,128]{2,1,0:T(8,128)(2,1)S(1)}, u32[]{:S(2)}, u32[]{:S(2)}) async-start(bf16[32,24,128]{2,1,0:T(8,128)(2,1)} %copy.50), calls=%async_computation.3 | async-start | bytes 393216 | tf_op jit(solution)/shard_map/all_to_all | solution.py:101
  79.7 9.0 %collective-permute-start = (bf16[256,1,128]{2,0,1:T(8,128)(2,1)}, bf16[256,1,128]{2,0,1:T(8,128)(2,1)S(1)}, u32[]{:S(2)}, u32[]{:S(2)}) collective-permute-start(bf16[256,1,128]{2,0,1:T(8,128)(2,1)} %copy.74), channel_id=1, source_target_pairs={{0,1},{1,2},{2,3},{3,4},{4,5},{5,6},{6,7},{7,8},{8,9},{9,10},{10,1... | collective-permute-start | bytes 196616 | tf_op jit(solution)/shard_map/while/body/eval_jaxpr/ppermute | solution.py:17
  89.3 9.2 %collective-permute-start = (bf16[256,1,128]{2,0,1:T(8,128)(2,1)}, bf16[256,1,128]{2,0,1:T(8,128)(2,1)S(1)}, u32[]{:S(2)}, u32[]{:S(2)}) collective-permute-start(bf16[256,1,128]{2,0,1:T(8,128)(2,1)} %copy.74), channel_id=1, source_target_pairs={{0,1},{1,2},{2,3},{3,4},{4,5},{5,6},{6,7},{7,8},{8,9},{9,10},{10,1... | collective-permute-start | bytes 196616 | tf_op jit(solution)/shard_map/while/body/eval_jaxpr/ppermute | solution.py:17
  99.2 9.2 %collective-permute-start = (bf16[256,1,128]{2,0,1:T(8,128)(2,1)}, bf16[256,1,128]{2,0,1:T(8,128)(2,1)S(1)}, u32[]{:S(2)}, u32[]{:S(2)}) collective-permute-start(bf16[256,1,128]{2,0,1:T(8,128)(2,1)} %copy.74), channel_id=1, source_target_pairs={{0,1},{1,2},{2,3},{3,4},{4,5},{5,6},{6,7},{7,8},{8,9},{9,10},{10,1... | collective-permute-start | bytes 196616 | tf_op jit(solution)/shard_map/while/body/eval_jaxpr/ppermute | solution.py:17
  109.0 9.2 %collective-permute-start = (bf16[256,1,128]{2,0,1:T(8,128)(2,1)}, bf16[256,1,128]{2,0,1:T(8,128)(2,1)S(1)}, u32[]{:S(2)}, u32[]{:S(2)}) collective-permute-start(bf16[256,1,128]{2,0,1:T(8,128)(2,1)} %copy.74), channel_id=1, source_target_pairs={{0,1},{1,2},{2,3},{3,4},{4,5},{5,6},{6,7},{7,8},{8,9},{9,10},{10,1... | collective-permute-start | bytes 196616 | tf_op jit(solution)/shard_map/while/body/eval_jaxpr/ppermute | solution.py:17
  167.7 8.9 %collective-permute-start = (bf16[256,1,128]{2,0,1:T(8,128)(2,1)}, bf16[256,1,128]{2,0,1:T(8,128)(2,1)S(1)}, u32[]{:S(2)}, u32[]{:S(2)}) collective-permute-start(bf16[256,1,128]{2,0,1:T(8,128)(2,1)} %copy.74), channel_id=1, source_target_pairs={{0,1},{1,2},{2,3},{3,4},{4,5},{5,6},{6,7},{7,8},{8,9},{9,10},{10,1... | collective-permute-start | bytes 196616 | tf_op jit(solution)/shard_map/while/body/eval_jaxpr/ppermute | solution.py:17
  189.1 8.9 %collective-permute-start = (bf16[256,1,128]{2,0,1:T(8,128)(2,1)}, bf16[256,1,128]{2,0,1:T(8,128)(2,1)S(1)}, u32[]{:S(2)}, u32[]{:S(2)}) collective-permute-start(bf16[256,1,128]{2,0,1:T(8,128)(2,1)} %copy.74), channel_id=1, source_target_pairs={{0,1},{1,2},{2,3},{3,4},{4,5},{5,6},{6,7},{7,8},{8,9},{9,10},{10,1... | collective-permute-start | bytes 196616 | tf_op jit(solution)/shard_map/while/body/eval_jaxpr/ppermute | solution.py:17
  200.1 8.9 %collective-permute-start = (bf16[256,1,128]{2,0,1:T(8,128)(2,1)}, bf16[256,1,128]{2,0,1:T(8,128)(2,1)S(1)}, u32[]{:S(2)}, u32[]{:S(2)}) collective-permute-start(bf16[256,1,128]{2,0,1:T(8,128)(2,1)} %copy.74), channel_id=1, source_target_pairs={{0,1},{1,2},{2,3},{3,4},{4,5},{5,6},{6,7},{7,8},{8,9},{9,10},{10,1... | collective-permute-start | bytes 196616 | tf_op jit(solution)/shard_map/while/body/eval_jaxpr/ppermute | solution.py:17
  221.5 8.9 %collective-permute-start = (bf16[256,1,128]{2,0,1:T(8,128)(2,1)}, bf16[256,1,128]{2,0,1:T(8,128)(2,1)S(1)}, u32[]{:S(2)}, u32[]{:S(2)}) collective-permute-start(bf16[256,1,128]{2,0,1:T(8,128)(2,1)} %copy.74), channel_id=1, source_target_pairs={{0,1},{1,2},{2,3},{3,4},{4,5},{5,6},{6,7},{7,8},{8,9},{9,10},{10,1... | collective-permute-start | bytes 196616 | tf_op jit(solution)/shard_map/while/body/eval_jaxpr/ppermute | solution.py:17
  232.6 8.9 %collective-permute-start = (bf16[256,1,128]{2,0,1:T(8,128)(2,1)}, bf16[256,1,128]{2,0,1:T(8,128)(2,1)S(1)}, u32[]{:S(2)}, u32[]{:S(2)}) collective-permute-start(bf16[256,1,128]{2,0,1:T(8,128)(2,1)} %copy.74), channel_id=1, source_target_pairs={{0,1},{1,2},{2,3},{3,4},{4,5},{5,6},{6,7},{7,8},{8,9},{9,10},{10,1... | collective-permute-start | bytes 196616 | tf_op jit(solution)/shard_map/while/body/eval_jaxpr/ppermute | solution.py:17
  254.0 8.9 %collective-permute-start = (bf16[256,1,128]{2,0,1:T(8,128)(2,1)}, bf16[256,1,128]{2,0,1:T(8,128)(2,1)S(1)}, u32[]{:S(2)}, u32[]{:S(2)}) collective-permute-start(bf16[256,1,128]{2,0,1:T(8,128)(2,1)} %copy.74), channel_id=1, source_target_pairs={{0,1},{1,2},{2,3},{3,4},{4,5},{5,6},{6,7},{7,8},{8,9},{9,10},{10,1... | collective-permute-start | bytes 196616 | tf_op jit(solution)/shard_map/while/body/eval_jaxpr/ppermute | solution.py:17
  265.1 8.9 %collective-permute-start = (bf16[256,1,128]{2,0,1:T(8,128)(2,1)}, bf16[256,1,128]{2,0,1:T(8,128)(2,1)S(1)}, u32[]{:S(2)}, u32[]{:S(2)}) collective-permute-start(bf16[256,1,128]{2,0,1:T(8,128)(2,1)} %copy.74), channel_id=1, source_target_pairs={{0,1},{1,2},{2,3},{3,4},{4,5},{5,6},{6,7},{7,8},{8,9},{9,10},{10,1... | collective-permute-start | bytes 196616 | tf_op jit(solution)/shard_map/while/body/eval_jaxpr/ppermute | solution.py:17
  286.5 8.9 %collective-permute-start = (bf16[256,1,128]{2,0,1:T(8,128)(2,1)}, bf16[256,1,128]{2,0,1:T(8,128)(2,1)S(1)}, u32[]{:S(2)}, u32[]{:S(2)}) collective-permute-start(bf16[256,1,128]{2,0,1:T(8,128)(2,1)} %copy.74), channel_id=1, source_target_pairs={{0,1},{1,2},{2,3},{3,4},{4,5},{5,6},{6,7},{7,8},{8,9},{9,10},{10,1... | collective-permute-start | bytes 196616 | tf_op jit(solution)/shard_map/while/body/eval_jaxpr/ppermute | solution.py:17
  297.5 8.9 %collective-permute-start = (bf16[256,1,128]{2,0,1:T(8,128)(2,1)}, bf16[256,1,128]{2,0,1:T(8,128)(2,1)S(1)}, u32[]{:S(2)}, u32[]{:S(2)}) collective-permute-start(bf16[256,1,128]{2,0,1:T(8,128)(2,1)} %copy.74), channel_id=1, source_target_pairs={{0,1},{1,2},{2,3},{3,4},{4,5},{5,6},{6,7},{7,8},{8,9},{9,10},{10,1... | collective-permute-start | bytes 196616 | tf_op jit(solution)/shard_map/while/body/eval_jaxpr/ppermute | solution.py:17
  308.6 8.9 %collective-permute-start = (bf16[256,1,128]{2,0,1:T(8,128)(2,1)}, bf16[256,1,128]{2,0,1:T(8,128)(2,1)S(1)}, u32[]{:S(2)}, u32[]{:S(2)}) collective-permute-start(bf16[256,1,128]{2,0,1:T(8,128)(2,1)} %copy.74), channel_id=1, source_target_pairs={{0,1},{1,2},{2,3},{3,4},{4,5},{5,6},{6,7},{7,8},{8,9},{9,10},{10,1... | collective-permute-start | bytes 196616 | tf_op jit(solution)/shard_map/while/body/eval_jaxpr/ppermute | solution.py:17
  319.7 8.9 %collective-permute-start = (bf16[256,1,128]{2,0,1:T(8,128)(2,1)}, bf16[256,1,128]{2,0,1:T(8,128)(2,1)S(1)}, u32[]{:S(2)}, u32[]{:S(2)}) collective-permute-start(bf16[256,1,128]{2,0,1:T(8,128)(2,1)} %copy.74), channel_id=1, source_target_pairs={{0,1},{1,2},{2,3},{3,4},{4,5},{5,6},{6,7},{7,8},{8,9},{9,10},{10,1... | collective-permute-start | bytes 196616 | tf_op jit(solution)/shard_map/while/body/eval_jaxpr/ppermute | solution.py:17
  330.7 8.9 %collective-permute-start = (bf16[256,1,128]{2,0,1:T(8,128)(2,1)}, bf16[256,1,128]{2,0,1:T(8,128)(2,1)S(1)}, u32[]{:S(2)}, u32[]{:S(2)}) collective-permute-start(bf16[256,1,128]{2,0,1:T(8,128)(2,1)} %copy.74), channel_id=1, source_target_pairs={{0,1},{1,2},{2,3},{3,4},{4,5},{5,6},{6,7},{7,8},{8,9},{9,10},{10,1... | collective-permute-start | bytes 196616 | tf_op jit(solution)/shard_map/while/body/eval_jaxpr/ppermute | solution.py:17
  341.8 8.9 %collective-permute-start = (bf16[256,1,128]{2,0,1:T(8,128)(2,1)}, bf16[256,1,128]{2,0,1:T(8,128)(2,1)S(1)}, u32[]{:S(2)}, u32[]{:S(2)}) collective-permute-start(bf16[256,1,128]{2,0,1:T(8,128)(2,1)} %copy.74), channel_id=1, source_target_pairs={{0,1},{1,2},{2,3},{3,4},{4,5},{5,6},{6,7},{7,8},{8,9},{9,10},{10,1... | collective-permute-start | bytes 196616 | tf_op jit(solution)/shard_map/while/body/eval_jaxpr/ppermute | solution.py:17
  352.9 8.9 %collective-permute-start = (bf16[256,1,128]{2,0,1:T(8,128)(2,1)}, bf16[256,1,128]{2,0,1:T(8,128)(2,1)S(1)}, u32[]{:S(2)}, u32[]{:S(2)}) collective-permute-start(bf16[256,1,128]{2,0,1:T(8,128)(2,1)} %copy.74), channel_id=1, source_target_pairs={{0,1},{1,2},{2,3},{3,4},{4,5},{5,6},{6,7},{7,8},{8,9},{9,10},{10,1... | collective-permute-start | bytes 196616 | tf_op jit(solution)/shard_map/while/body/eval_jaxpr/ppermute | solution.py:17
  364.0 8.9 %collective-permute-start = (bf16[256,1,128]{2,0,1:T(8,128)(2,1)}, bf16[256,1,128]{2,0,1:T(8,128)(2,1)S(1)}, u32[]{:S(2)}, u32[]{:S(2)}) collective-permute-start(bf16[256,1,128]{2,0,1:T(8,128)(2,1)} %copy.74), channel_id=1, source_target_pairs={{0,1},{1,2},{2,3},{3,4},{4,5},{5,6},{6,7},{7,8},{8,9},{9,10},{10,1... | collective-permute-start | bytes 196616 | tf_op jit(solution)/shard_map/while/body/eval_jaxpr/ppermute | solution.py:17
  375.0 8.9 %collective-permute-start = (bf16[256,1,128]{2,0,1:T(8,128)(2,1)}, bf16[256,1,128]{2,0,1:T(8,128)(2,1)S(1)}, u32[]{:S(2)}, u32[]{:S(2)}) collective-permute-start(bf16[256,1,128]{2,0,1:T(8,128)(2,1)} %copy.74), channel_id=1, source_target_pairs={{0,1},{1,2},{2,3},{3,4},{4,5},{5,6},{6,7},{7,8},{8,9},{9,10},{10,1... | collective-permute-start | bytes 196616 | tf_op jit(solution)/shard_map/while/body/eval_jaxpr/ppermute | solution.py:17
  386.7 12.7 %collective-permute-start.4 = (f32[256,1,128]{2,0,1:T(8,128)S(1)}, f32[256,1,128]{2,0,1:T(8,128)S(1)}, u32[]{:S(2)}, u32[]{:S(2)}) collective-permute-start(f32[256,1,128]{2,0,1:T(8,128)S(1)} %get-tuple-element.1072), channel_id=1, source_target_pairs={{0,1},{1,2},{2,3},{3,4},{4,5},{5,6},{6,7},{7,8},{8,9},{9,10},{10,1... | collective-permute-start | bytes 393224 | tf_op jit(solution)/shard_map/while/body/eval_jaxpr/ppermute | solution.py:22
  389.4 10.0 %collective-permute-start.5 = (f32[256,1,128]{2,0,1:T(8,128)S(1)}, f32[256,1,128]{2,0,1:T(8,128)S(1)}, u32[]{:S(2)}, u32[]{:S(2)}) collective-permute-start(f32[256,1,128]{2,0,1:T(8,128)S(1)} %get-tuple-element.1073), channel_id=1, source_target_pairs={{0,1},{1,2},{2,3},{3,4},{4,5},{5,6},{6,7},{7,8},{8,9},{9,10},{10,1... | collective-permute-start | bytes 393224 | tf_op jit(solution)/shard_map/while/body/eval_jaxpr/ppermute | solution.py:22
  401.9 12.6 %collective-permute-start.4 = (f32[256,1,128]{2,0,1:T(8,128)S(1)}, f32[256,1,128]{2,0,1:T(8,128)S(1)}, u32[]{:S(2)}, u32[]{:S(2)}) collective-permute-start(f32[256,1,128]{2,0,1:T(8,128)S(1)} %get-tuple-element.1072), channel_id=1, source_target_pairs={{0,1},{1,2},{2,3},{3,4},{4,5},{5,6},{6,7},{7,8},{8,9},{9,10},{10,1... | collective-permute-start | bytes 393224 | tf_op jit(solution)/shard_map/while/body/eval_jaxpr/ppermute | solution.py:22
  404.3 10.2 %collective-permute-start.5 = (f32[256,1,128]{2,0,1:T(8,128)S(1)}, f32[256,1,128]{2,0,1:T(8,128)S(1)}, u32[]{:S(2)}, u32[]{:S(2)}) collective-permute-start(f32[256,1,128]{2,0,1:T(8,128)S(1)} %get-tuple-element.1073), channel_id=1, source_target_pairs={{0,1},{1,2},{2,3},{3,4},{4,5},{5,6},{6,7},{7,8},{8,9},{9,10},{10,1... | collective-permute-start | bytes 393224 | tf_op jit(solution)/shard_map/while/body/eval_jaxpr/ppermute | solution.py:22
  417.0 12.7 %collective-permute-start.4 = (f32[256,1,128]{2,0,1:T(8,128)S(1)}, f32[256,1,128]{2,0,1:T(8,128)S(1)}, u32[]{:S(2)}, u32[]{:S(2)}) collective-permute-start(f32[256,1,128]{2,0,1:T(8,128)S(1)} %get-tuple-element.1072), channel_id=1, source_target_pairs={{0,1},{1,2},{2,3},{3,4},{4,5},{5,6},{6,7},{7,8},{8,9},{9,10},{10,1... | collective-permute-start | bytes 393224 | tf_op jit(solution)/shard_map/while/body/eval_jaxpr/ppermute | solution.py:22
  420.0 9.7 %collective-permute-start.5 = (f32[256,1,128]{2,0,1:T(8,128)S(1)}, f32[256,1,128]{2,0,1:T(8,128)S(1)}, u32[]{:S(2)}, u32[]{:S(2)}) collective-permute-start(f32[256,1,128]{2,0,1:T(8,128)S(1)} %get-tuple-element.1073), channel_id=1, source_target_pairs={{0,1},{1,2},{2,3},{3,4},{4,5},{5,6},{6,7},{7,8},{8,9},{9,10},{10,1... | collective-permute-start | bytes 393224 | tf_op jit(solution)/shard_map/while/body/eval_jaxpr/ppermute | solution.py:22
  432.2 9.7 %collective-permute-start.4 = (f32[256,1,128]{2,0,1:T(8,128)S(1)}, f32[256,1,128]{2,0,1:T(8,128)S(1)}, u32[]{:S(2)}, u32[]{:S(2)}) collective-permute-start(f32[256,1,128]{2,0,1:T(8,128)S(1)} %get-tuple-element.1072), channel_id=1, source_target_pairs={{0,1},{1,2},{2,3},{3,4},{4,5},{5,6},{6,7},{7,8},{8,9},{9,10},{10,1... | collective-permute-start | bytes 393224 | tf_op jit(solution)/shard_map/while/body/eval_jaxpr/ppermute | solution.py:22
  444.4 9.7 %collective-permute-start.4 = (f32[256,1,128]{2,0,1:T(8,128)S(1)}, f32[256,1,128]{2,0,1:T(8,128)S(1)}, u32[]{:S(2)}, u32[]{:S(2)}) collective-permute-start(f32[256,1,128]{2,0,1:T(8,128)S(1)} %get-tuple-element.1072), channel_id=1, source_target_pairs={{0,1},{1,2},{2,3},{3,4},{4,5},{5,6},{6,7},{7,8},{8,9},{9,10},{10,1... | collective-permute-start | bytes 393224 | tf_op jit(solution)/shard_map/while/body/eval_jaxpr/ppermute | solution.py:22
  456.5 8.5 %collective-permute-start.4 = (f32[256,1,128]{2,0,1:T(8,128)S(1)}, f32[256,1,128]{2,0,1:T(8,128)S(1)}, u32[]{:S(2)}, u32[]{:S(2)}) collective-permute-start(f32[256,1,128]{2,0,1:T(8,128)S(1)} %get-tuple-element.1072), channel_id=1, source_target_pairs={{0,1},{1,2},{2,3},{3,4},{4,5},{5,6},{6,7},{7,8},{8,9},{9,10},{10,1... | collective-permute-start | bytes 393224 | tf_op jit(solution)/shard_map/while/body/eval_jaxpr/ppermute | solution.py:22
  466.4 9.6 %collective-permute-start.4 = (f32[256,1,128]{2,0,1:T(8,128)S(1)}, f32[256,1,128]{2,0,1:T(8,128)S(1)}, u32[]{:S(2)}, u32[]{:S(2)}) collective-permute-start(f32[256,1,128]{2,0,1:T(8,128)S(1)} %get-tuple-element.1072), channel_id=1, source_target_pairs={{0,1},{1,2},{2,3},{3,4},{4,5},{5,6},{6,7},{7,8},{8,9},{9,10},{10,1... | collective-permute-start | bytes 393224 | tf_op jit(solution)/shard_map/while/body/eval_jaxpr/ppermute | solution.py:22
  477.3 9.6 %collective-permute-start.4 = (f32[256,1,128]{2,0,1:T(8,128)S(1)}, f32[256,1,128]{2,0,1:T(8,128)S(1)}, u32[]{:S(2)}, u32[]{:S(2)}) collective-permute-start(f32[256,1,128]{2,0,1:T(8,128)S(1)} %get-tuple-element.1072), channel_id=1, source_target_pairs={{0,1},{1,2},{2,3},{3,4},{4,5},{5,6},{6,7},{7,8},{8,9},{9,10},{10,1... | collective-permute-start | bytes 393224 | tf_op jit(solution)/shard_map/while/body/eval_jaxpr/ppermute | solution.py:22
  488.3 9.6 %collective-permute-start.4 = (f32[256,1,128]{2,0,1:T(8,128)S(1)}, f32[256,1,128]{2,0,1:T(8,128)S(1)}, u32[]{:S(2)}, u32[]{:S(2)}) collective-permute-start(f32[256,1,128]{2,0,1:T(8,128)S(1)} %get-tuple-element.1072), channel_id=1, source_target_pairs={{0,1},{1,2},{2,3},{3,4},{4,5},{5,6},{6,7},{7,8},{8,9},{9,10},{10,1... | collective-permute-start | bytes 393224 | tf_op jit(solution)/shard_map/while/body/eval_jaxpr/ppermute | solution.py:22
  499.3 8.5 %collective-permute-start.4 = (f32[256,1,128]{2,0,1:T(8,128)S(1)}, f32[256,1,128]{2,0,1:T(8,128)S(1)}, u32[]{:S(2)}, u32[]{:S(2)}) collective-permute-start(f32[256,1,128]{2,0,1:T(8,128)S(1)} %get-tuple-element.1072), channel_id=1, source_target_pairs={{0,1},{1,2},{2,3},{3,4},{4,5},{5,6},{6,7},{7,8},{8,9},{9,10},{10,1... | collective-permute-start | bytes 393224 | tf_op jit(solution)/shard_map/while/body/eval_jaxpr/ppermute | solution.py:22
  509.1 9.6 %collective-permute-start.4 = (f32[256,1,128]{2,0,1:T(8,128)S(1)}, f32[256,1,128]{2,0,1:T(8,128)S(1)}, u32[]{:S(2)}, u32[]{:S(2)}) collective-permute-start(f32[256,1,128]{2,0,1:T(8,128)S(1)} %get-tuple-element.1072), channel_id=1, source_target_pairs={{0,1},{1,2},{2,3},{3,4},{4,5},{5,6},{6,7},{7,8},{8,9},{9,10},{10,1... | collective-permute-start | bytes 393224 | tf_op jit(solution)/shard_map/while/body/eval_jaxpr/ppermute | solution.py:22
  520.1 9.6 %collective-permute-start.4 = (f32[256,1,128]{2,0,1:T(8,128)S(1)}, f32[256,1,128]{2,0,1:T(8,128)S(1)}, u32[]{:S(2)}, u32[]{:S(2)}) collective-permute-start(f32[256,1,128]{2,0,1:T(8,128)S(1)} %get-tuple-element.1072), channel_id=1, source_target_pairs={{0,1},{1,2},{2,3},{3,4},{4,5},{5,6},{6,7},{7,8},{8,9},{9,10},{10,1... | collective-permute-start | bytes 393224 | tf_op jit(solution)/shard_map/while/body/eval_jaxpr/ppermute | solution.py:22
  540.9 9.6 %collective-permute-start.4 = (f32[256,1,128]{2,0,1:T(8,128)S(1)}, f32[256,1,128]{2,0,1:T(8,128)S(1)}, u32[]{:S(2)}, u32[]{:S(2)}) collective-permute-start(f32[256,1,128]{2,0,1:T(8,128)S(1)} %get-tuple-element.1072), channel_id=1, source_target_pairs={{0,1},{1,2},{2,3},{3,4},{4,5},{5,6},{6,7},{7,8},{8,9},{9,10},{10,1... | collective-permute-start | bytes 393224 | tf_op jit(solution)/shard_map/while/body/eval_jaxpr/ppermute | solution.py:22
  551.9 9.6 %collective-permute-start.4 = (f32[256,1,128]{2,0,1:T(8,128)S(1)}, f32[256,1,128]{2,0,1:T(8,128)S(1)}, u32[]{:S(2)}, u32[]{:S(2)}) collective-permute-start(f32[256,1,128]{2,0,1:T(8,128)S(1)} %get-tuple-element.1072), channel_id=1, source_target_pairs={{0,1},{1,2},{2,3},{3,4},{4,5},{5,6},{6,7},{7,8},{8,9},{9,10},{10,1... | collective-permute-start | bytes 393224 | tf_op jit(solution)/shard_map/while/body/eval_jaxpr/ppermute | solution.py:22
  562.9 8.5 %collective-permute-start.4 = (f32[256,1,128]{2,0,1:T(8,128)S(1)}, f32[256,1,128]{2,0,1:T(8,128)S(1)}, u32[]{:S(2)}, u32[]{:S(2)}) collective-permute-start(f32[256,1,128]{2,0,1:T(8,128)S(1)} %get-tuple-element.1072), channel_id=1, source_target_pairs={{0,1},{1,2},{2,3},{3,4},{4,5},{5,6},{6,7},{7,8},{8,9},{9,10},{10,1... | collective-permute-start | bytes 393224 | tf_op jit(solution)/shard_map/while/body/eval_jaxpr/ppermute | solution.py:22
  572.7 9.6 %collective-permute-start.4 = (f32[256,1,128]{2,0,1:T(8,128)S(1)}, f32[256,1,128]{2,0,1:T(8,128)S(1)}, u32[]{:S(2)}, u32[]{:S(2)}) collective-permute-start(f32[256,1,128]{2,0,1:T(8,128)S(1)} %get-tuple-element.1072), channel_id=1, source_target_pairs={{0,1},{1,2},{2,3},{3,4},{4,5},{5,6},{6,7},{7,8},{8,9},{9,10},{10,1... | collective-permute-start | bytes 393224 | tf_op jit(solution)/shard_map/while/body/eval_jaxpr/ppermute | solution.py:22
  583.7 9.6 %collective-permute-start.4 = (f32[256,1,128]{2,0,1:T(8,128)S(1)}, f32[256,1,128]{2,0,1:T(8,128)S(1)}, u32[]{:S(2)}, u32[]{:S(2)}) collective-permute-start(f32[256,1,128]{2,0,1:T(8,128)S(1)} %get-tuple-element.1072), channel_id=1, source_target_pairs={{0,1},{1,2},{2,3},{3,4},{4,5},{5,6},{6,7},{7,8},{8,9},{9,10},{10,1... | collective-permute-start | bytes 393224 | tf_op jit(solution)/shard_map/while/body/eval_jaxpr/ppermute | solution.py:22
  604.5 9.6 %collective-permute-start.4 = (f32[256,1,128]{2,0,1:T(8,128)S(1)}, f32[256,1,128]{2,0,1:T(8,128)S(1)}, u32[]{:S(2)}, u32[]{:S(2)}) collective-permute-start(f32[256,1,128]{2,0,1:T(8,128)S(1)} %get-tuple-element.1072), channel_id=1, source_target_pairs={{0,1},{1,2},{2,3},{3,4},{4,5},{5,6},{6,7},{7,8},{8,9},{9,10},{10,1... | collective-permute-start | bytes 393224 | tf_op jit(solution)/shard_map/while/body/eval_jaxpr/ppermute | solution.py:22
  615.5 9.6 %collective-permute-start.4 = (f32[256,1,128]{2,0,1:T(8,128)S(1)}, f32[256,1,128]{2,0,1:T(8,128)S(1)}, u32[]{:S(2)}, u32[]{:S(2)}) collective-permute-start(f32[256,1,128]{2,0,1:T(8,128)S(1)} %get-tuple-element.1072), channel_id=1, source_target_pairs={{0,1},{1,2},{2,3},{3,4},{4,5},{5,6},{6,7},{7,8},{8,9},{9,10},{10,1... | collective-permute-start | bytes 393224 | tf_op jit(solution)/shard_map/while/body/eval_jaxpr/ppermute | solution.py:22
  646.2 8.5 %collective-permute-start.4 = (f32[256,1,128]{2,0,1:T(8,128)S(1)}, f32[256,1,128]{2,0,1:T(8,128)S(1)}, u32[]{:S(2)}, u32[]{:S(2)}) collective-permute-start(f32[256,1,128]{2,0,1:T(8,128)S(1)} %get-tuple-element.1072), channel_id=1, source_target_pairs={{0,1},{1,2},{2,3},{3,4},{4,5},{5,6},{6,7},{7,8},{8,9},{9,10},{10,1... | collective-permute-start | bytes 393224 | tf_op jit(solution)/shard_map/while/body/eval_jaxpr/ppermute | solution.py:22
  656.0 8.5 %collective-permute-start.4 = (f32[256,1,128]{2,0,1:T(8,128)S(1)}, f32[256,1,128]{2,0,1:T(8,128)S(1)}, u32[]{:S(2)}, u32[]{:S(2)}) collective-permute-start(f32[256,1,128]{2,0,1:T(8,128)S(1)} %get-tuple-element.1072), channel_id=1, source_target_pairs={{0,1},{1,2},{2,3},{3,4},{4,5},{5,6},{6,7},{7,8},{8,9},{9,10},{10,1... | collective-permute-start | bytes 393224 | tf_op jit(solution)/shard_map/while/body/eval_jaxpr/ppermute | solution.py:22
  (149 other events, 825.1 us)
where the time goes:
time: 741 us; the launch traced here: 731 us
  starting transfers between devices  551 us (74%)
  waiting for transfers between devices  99.1 us (13%)
  local copies, waits for them, and re-layouts  53.4 us (7%)
  matrix products  19.4 us (3%)
    ppermute x124, starting transfers between devices, from_behind(): return lax.ppermute(x, axis, pairs)  434 us
    ppermute x64, starting transfers between devices, from_behind_2(): lax.ppermute(x, axis, [(i, (i + by) % devices) for i in range(devices)])  87.7 us
    ppermute x124, waiting for transfers between devices, from_behind(): return lax.ppermute(x, axis, pairs)  78.5 us
    another operation x124, local copies, waits for them, and re-layouts  39.4 us
  transfers between devices with their start and end apart: 192, of which 62 were waited for; matrix products, arithmetic and copies ran while one was open for 6% of the time, Pallas kernels for 0%

commit v1 on v0

v1 whole, which is shorter than its diff:
```python
import functools
import math

import jax
import jax.numpy as jnp
from jax import lax
from jax.experimental import pallas as pl
from jax.experimental.pallas import tpu as pltpu
from jax.sharding import PartitionSpec as P

DH = 128
CAP = 3
GROUP = 8
CHUNK = 512
MASKED = -1e30
MESH = pl.DeviceIdType.MESH
F32 = jnp.float32
BF16 = jnp.bfloat16


def dot_nt(a, b):
    return lax.dot_general(a, b, (((1,), (1,)), ((), ())), preferred_element_type=F32)


def dot_nn(a, b):
    return lax.dot_general(a, b, (((1,), (0,)), ((), ())), preferred_element_type=F32)


def iota(shape, dim):
    return lax.broadcasted_iota(jnp.int32, shape, dim)


def kernel(heads, ctxs, group, *refs):
    (q_hbm, k_hbm, v_hbm, t_hbm, slots_hbm, spans_hbm, dq_ref, dk_ref, dv_ref) = refs[:9]
    (slots_in, spans_in, hop1_out, hop1_in, hop2_out, hop2_in) = refs[9:15]
    (qg, dog, kb, vb, kt, pt, p16, dp, mrow, lse_st, del_st, drow) = refs[15:27]
    (dqa, dq_out, dq_sib, dq_far, dq_in) = refs[27:32]
    (dk_out, dk_in, dk_own, dv_out, dv_in, dv_own) = refs[32:38]
    (in_sem, h_send, h_recv, c_send, c_recv, q_send, q_recv, k_send, k_recv) = refs[38:47]
    (v_send, v_recv, do_send, do_recv, l_send, l_recv, d_send, d_recv) = refs[47:55]
    (s_send, s_recv, dq_send, dq_recv, dk_send, dk_recv, dv_send, dv_recv) = refs[55:63]
    me_h = lax.axis_index("head")
    me_c = lax.axis_index("ctx")
    z = lax.div(me_c, group)
    r = lax.rem(me_c, group)
    base = z * group
    core = lax.rem(r, 2)
    chip = lax.div(r, 2)
    chips = group // 2
    sibling = r + 1 - 2 * core
    rows = dq_ref.shape[0]
    trows = t_hbm.shape[0]
    lines = ctxs // group
    chunks = group * rows // CHUNK
    per_chunk = CHUNK // rows
    scale = 1.0 / math.sqrt(DH)

    def each(start, stop, f):
        def body(i, carry):
            f(i)
            return carry

        lax.fori_loop(start, stop, body, 0)

    def group_peer(i):
        return lax.rem(r + i, group)

    def far_peer(i):
        return lax.rem(r + 2 * i, group)

    def block(index):
        return pl.ds(pl.multiple_of(index * rows, rows), rows)

    def remote(src, dst, send, recv, device):
        return pltpu.make_async_remote_copy(
            src_ref=src,
            dst_ref=dst,
            send_sem=send,
            recv_sem=recv,
            device_id=device,
            device_id_type=MESH,
        )

    def hop1(i):
        peer = lax.rem(me_h + i, heads)
        return remote(
            hop1_out.at[peer], hop1_in.at[me_h], h_send.at[i], h_recv.at[me_h], (peer, me_c)
        )

    def hop1_arrival(i):
        peer = lax.rem(me_h + i, heads)
        return remote(
            hop1_out.at[peer], hop1_in.at[peer], h_send.at[i], h_recv.at[peer], (peer, me_c)
        )

    def hop2(i):
        peer = lax.rem(me_c + i, ctxs)
        return remote(
            hop2_out.at[peer], hop2_in.at[me_c], c_send.at[i], c_recv.at[me_c], (me_h, peer)
        )

    def hop2_arrival(i):
        peer = lax.rem(me_c + i, ctxs)
        return remote(
            hop2_out.at[peer], hop2_in.at[peer], c_send.at[i], c_recv.at[peer], (me_h, peer)
        )

    def share(buffer, send, recv, which, index, peer):
        here = buffer.at[block(which), :]
        return remote(here, here, send.at[index], recv.at[which], (me_h, base + peer))

    def share_far(buffer, send, recv, i):
        return share(buffer, send, recv, r, i, far_peer(i))

    def share_near(buffer, send, recv):
        return share(buffer, send, recv, r, 0, sibling)

    def share_on(buffer, send, recv, i):
        return share(buffer, send, recv, far_peer(i), chips + i, sibling)

    def share_start(buffer, send, recv):
        each(1, chips, lambda i: share_far(buffer, send, recv, i).start())
        share_near(buffer, send, recv).start()

    def share_forward(buffer, send, recv):
        def step(i):
            share(buffer, send, recv, far_peer(i), i, far_peer(i)).wait_recv()
            share_on(buffer, send, recv, i).start()

        each(1, chips, step)

    def share_sent(buffer, send, recv):
        share_near(buffer, send, recv).wait_send()

        def step(i):
            share_far(buffer, send, recv, i).wait_send()
            share_on(buffer, send, recv, i).wait_send()

        each(1, chips, step)

    def to_line(buffer, send, recv, line):
        return remote(
            buffer.at[z], buffer.at[z], send.at[line], recv.at[z], (me_h, line * group + r)
        )

    def from_line(buffer, send, recv, line):
        return remote(
            buffer.at[line],
            buffer.at[line],
            send.at[line],
            recv.at[line],
            (me_h, line * group + r),
        )

    def stat(buffer, send, recv, i):
        return remote(
            buffer.at[r], buffer.at[r], send.at[i], recv.at[r], (me_h, base + group_peer(i))
        )

    def stat_arrival(buffer, send, recv, i):
        src = group_peer(i)
        return remote(
            buffer.at[src], buffer.at[src], send.at[i], recv.at[src], (me_h, base + src)
        )

    def back(out, landing, send, recv, line):
        return remote(
            out.at[line], landing.at[z], send.at[line], recv.at[z], (me_h, line * group + r)
        )

    def back_arrival(out, landing, send, recv, line):
        return remote(
            out.at[line], landing.at[line], send.at[line], recv.at[line], (me_h, line * group + r)
        )

    def dq_near(j):
        there = 2 * j + 1 - core
        return remote(
            dq_out.at[there], dq_sib.at[j], s_send.at[j], s_recv.at[j], (me_h, base + sibling)
        )

    def dq_away(i):
        peer = far_peer(i)
        return remote(
            dq_far.at[lax.div(peer, 2)],
            dq_in.at[chip],
            dq_send.at[i],
            dq_recv.at[chip],
            (me_h, base + peer),
        )

    def dq_arrival(i):
        src = far_peer(i)
        return remote(
            dq_far.at[lax.div(src, 2)],
            dq_in.at[lax.div(src, 2)],
            dq_send.at[i],
            dq_recv.at[lax.div(src, 2)],
            (me_h, base + src),
        )

    barrier = pltpu.get_barrier_semaphore()

    def greet(device):
        pl.semaphore_signal(barrier, inc=1, device_id=device, device_id_type=MESH)

    each(1, heads, lambda i: greet((lax.rem(me_h + i, heads), me_c)))
    each(1, ctxs, lambda i: greet((me_h, lax.rem(me_c + i, ctxs))))

    loads = [
        pltpu.make_async_copy(slots_hbm, slots_in, in_sem.at[0]),
        pltpu.make_async_copy(spans_hbm, spans_in, in_sem.at[1]),
        pltpu.make_async_copy(q_hbm, qg.at[block(r), :], in_sem.at[2]),
        pltpu.make_async_copy(k_hbm, kb.at[z], in_sem.at[3]),
        pltpu.make_async_copy(v_hbm, vb.at[z], in_sem.at[4]),
    ]
    for h in range(heads):
        loads.append(
            pltpu.make_async_copy(
                t_hbm.at[:, h * DH : (h + 1) * DH], hop1_out.at[h, 0:trows, :], in_sem.at[5 + h]
            )
        )
    for load in loads:
        load.start()
    loads[0].wait()
    loads[1].wait()

    line16 = iota((16, trows), 0)
    slots = slots_in[...].astype(F32)
    spans = spans_in[...].astype(F32)
    meta = jnp.where(
        line16 == 0,
        slots,
        jnp.where(line16 == 1, spans[0:1], jnp.where(line16 == 2, spans[1:2], 0.0)),
    ).astype(BF16)
    place = jnp.bitwise_and(iota((trows, DH), 1), 63)
    pick = (place == iota((trows, DH), 0)).astype(F32).astype(BF16)
    meta = dot_nn(meta, pick)
    unused = (jnp.bitwise_and(iota((16, DH), 1), 63) >= trows) & (iota((16, DH), 0) == 0)
    meta = jnp.where(unused, -1.0, meta).astype(BF16)
    for h in range(heads):
        if trows < 48:
            hop1_out[h, trows:48, :] = jnp.zeros((48 - trows, DH), BF16)
        hop1_out[h, 48:64, :] = meta
    for load in loads[2:]:
        load.wait()

    pl.semaphore_wait(barrier, heads - 1 + ctxs - 1)

    each(1, heads, lambda i: hop1(i).start())
    hop1_in[me_h] = hop1_out[me_h]
    share_start(qg, q_send, q_recv)
    each(z + 1, lines, lambda line: to_line(kb, k_send, k_recv, line).start())
    each(1, heads, lambda i: hop1_arrival(i).wait_recv())

    kdepth = heads * 64
    teacher = hop1_in[...].reshape(kdepth, DH)
    eye = iota((64, DH), 0) == iota((64, DH), 1)
    ones = jnp.ones((DH, DH), BF16)
    firsts, lasts, codes = [], [], []
    lane1 = iota((1, DH), 1)
    for h in range(heads):
        tail = hop1_in[h, 48:64, :].astype(F32)
        firsts.append(jnp.where(eye, tail[1:2], 0.0).astype(BF16))
        lasts.append(jnp.where(eye, tail[2:3], 0.0).astype(BF16))
        codes.append(jnp.where(tail[0:1] < 0.0, -1.0, tail[0:1] + 128.0 * h))
    first = dot_nn(jnp.concatenate(firsts, axis=0), ones).astype(BF16)
    last = dot_nn(jnp.concatenate(lasts, axis=0), ones).astype(BF16)
    codes = [jnp.where(lane1 < 64, codes[h], codes[h + 1]) for h in range(0, heads, 2)]
    mine = lax.rem(me_c, 4) * 32

    def pack(step):
        row = iota((256, DH), 0)
        within = jnp.bitwise_and(row, 31)
        dest = lax.shift_right_logical(row, 5) + step * 8
        spot = lax.div(within, heads)
        head = within - spot * heads
        wanted = jnp.where(spot < CAP, dest * CAP + spot + 128 * head, -5).astype(F32)
        chosen = [(wanted == code).astype(F32).astype(BF16) for code in codes]
        chosen = jnp.concatenate(chosen, axis=1)
        moved = dot_nn(chosen, teacher).reshape(8, 32, DH)
        diagonal = (iota((256, DH), 1) == within + mine).astype(F32)
        lower = (dot_nn(chosen, first) * diagonal).reshape(8, 32, DH)
        upper = (dot_nn(chosen, last) * diagonal).reshape(8, 32, DH)
        lower = jnp.sum(lower, axis=1, keepdims=True)
        upper = jnp.sum(upper, axis=1, keepdims=True)
        line = iota((8, 8, DH), 1)
        tail = jnp.where(line == 0, lower, jnp.where(line == 1, upper, 0.0))
        message = jnp.concatenate([moved[:, 0:24, :], tail], axis=1)
        hop2_out[pl.ds(step * 8, 8)] = message.astype(BF16)

    each(0, ctxs // 8, pack)
    each(1, ctxs, lambda i: hop2(i).start())
    hop2_in[me_c] = hop2_out[me_c]
    each(z + 1, lines, lambda line: to_line(vb, v_send, v_recv, line).start())

    share_forward(qg, q_send, q_recv)

    def q_others(i):
        share(qg, q_send, q_recv, 2 * lax.rem(chip + i, chips) + 1 - core, 0, sibling).wait_recv()

    each(0, chips, q_others)
    each(0, z, lambda line: from_line(kb, k_send, k_recv, line).wait_recv())

    def transpose_keys(line):
        kt[line] = kb[line].astype(F32).T.astype(BF16)

    each(0, z + 1, transpose_keys)

    def scores_chunk(qc):
        queries = qg[pl.ds(pl.multiple_of(qc * CHUNK, CHUNK), CHUNK), :]

        def score(line, top):
            s = dot_nt(kb[line], queries)
            pt[line, qc] = s
            return jnp.maximum(top, jnp.max(s, axis=0, keepdims=True))

        top = lax.fori_loop(0, z, score, jnp.full((1, CHUNK), MASKED, F32))
        s = dot_nt(kb[z], queries)
        key_pos = iota((rows, CHUNK), 0) + r * rows
        query_pos = iota((rows, CHUNK), 1) + qc * CHUNK
        s = jnp.where(key_pos <= query_pos, s, MASKED)
        pt[z, qc] = s
        top = jnp.maximum(top, jnp.max(s, axis=0, keepdims=True))

        def weight(line, total):
            p = jnp.exp((pt[line, qc] - top) * scale)
            pt[line, qc] = p
            return total + jnp.sum(p, axis=0, keepdims=True)

        total = lax.fori_loop(0, z + 1, weight, jnp.zeros((1, CHUNK), F32))
        mrow[qc] = top * scale
        lse_st[r, qc] = top * scale + jnp.log(total)

    each(0, chunks, scores_chunk)
    each(1, group, lambda i: stat(lse_st, l_send, l_recv, i).start())
    each(1, group, lambda i: stat_arrival(lse_st, l_send, l_recv, i).wait_recv())

    def probs_chunk(qc):
        parts = lse_st[:, qc]
        top = jnp.max(parts, axis=0)
        lse = top + jnp.log(jnp.sum(jnp.exp(parts - top[None]), axis=0))
        fade = jnp.exp(mrow[qc] - lse)

        def fix(line):
            prob = pt[line, qc] * fade
            pt[line, qc] = prob
            p16[line, qc] = prob.astype(BF16)

        each(0, z + 1, fix)

    each(0, chunks, probs_chunk)

    each(1, ctxs, lambda i: hop2_arrival(i).wait_recv())
    token = iota((rows, DH), 0).astype(F32)

    def cover(step, total):
        four = hop2_in[pl.ds(step * 4, 4)]
        edges = jnp.sum(four[:, 16:32, :].astype(F32), axis=0)
        lower = edges[8:9]
        upper = edges[9:10]
        covered = jnp.where((token >= lower) & (token < upper), 1.0, 0.0).astype(BF16)
        return total + dot_nn(covered, four.reshape(4 * 32, DH))

    grad = lax.fori_loop(0, ctxs // 4, cover, jnp.zeros((rows, DH), F32))
    dog[block(r), :] = grad.astype(BF16)
    share_start(dog, do_send, do_recv)
    each(0, z, lambda line: from_line(vb, v_send, v_recv, line).wait_recv())

    def grad_probs(qc):
        grads = dog[pl.ds(pl.multiple_of(qc * CHUNK, CHUNK), CHUNK), :]

        def grad_prob(line, weighted):
            d = dot_nt(vb[line], grads)
            dp[line, qc] = d
            return weighted + jnp.sum(pt[line, qc] * d, axis=0, keepdims=True)

        del_st[r, qc] = lax.fori_loop(0, z + 1, grad_prob, jnp.zeros((1, CHUNK), F32))

    share(dog, do_send, do_recv, sibling, 0, sibling).wait_recv()
    grad_probs(chip)
    share_forward(dog, do_send, do_recv)

    def grad_others(i):
        there = lax.rem(chip + i, chips)
        share(dog, do_send, do_recv, 2 * there + 1 - core, 0, sibling).wait_recv()
        grad_probs(there)

    each(1, chips, grad_others)
    each(1, group, lambda i: stat(del_st, d_send, d_recv, i).start())

    def value_terms(line):
        total = jnp.zeros((rows, DH), F32)
        for qc in range(chunks):
            total += dot_nn(p16[line, qc], dog[qc * CHUNK : (qc + 1) * CHUNK, :])
        return total

    def earlier_values(line):
        dv_out[line] = value_terms(line).astype(BF16)
        back(dv_out, dv_in, dv_send, dv_recv, line).start()

    each(0, z, earlier_values)
    dv_own[...] = value_terms(z)

    each(1, group, lambda i: stat_arrival(del_st, d_send, d_recv, i).wait_recv())

    def deltas(qc):
        drow[qc] = jnp.sum(del_st[:, qc], axis=0)

    each(0, chunks, deltas)

    for b in range(group):
        dqa[b] = jnp.zeros((DH, rows), F32)

    def key_terms(line, last):
        key_sum = jnp.zeros((rows, DH), F32)
        for qc in range(chunks):
            dscore = (pt[line, qc] * (dp[line, qc] - drow[qc]) * scale).astype(BF16)
            key_sum += dot_nn(dscore, qg[qc * CHUNK : (qc + 1) * CHUNK, :])
            part = dot_nn(kt[line], dscore)
            for j in range(per_chunk):
                dqa[qc * per_chunk + j] += part[:, j * rows : (j + 1) * rows]
            if last:
                there = 2 * qc + 1 - core
                dq_out[there] = dqa[there].astype(BF16)
                dq_near(qc).start()
        return key_sum

    def earlier_keys(line):
        dk_out[line] = key_terms(line, False).astype(BF16)
        back(dk_out, dk_in, dk_send, dk_recv, line).start()

    each(0, z, earlier_keys)
    dk_own[...] = key_terms(z, True)

    def dq_join(i):
        here = lax.rem(chip + i, chips)
        dq_near(here).wait_recv()
        dq_far[here] = (dqa[2 * here + core] + dq_sib[here].astype(F32)).astype(BF16)
        dq_away(i).start()

    each(1, chips, dq_join)
    dq_near(chip).wait_recv()
    dq_total = dqa[r] + dq_sib[chip].astype(F32)

    def dv_add(line):
        back_arrival(dv_out, dv_in, dv_send, dv_recv, line).wait_recv()
        dv_own[...] += dv_in[line].astype(F32)

    each(z + 1, lines, dv_add)
    dv_ref[...] = dv_own[...].astype(BF16)

    def dk_add(line):
        back_arrival(dk_out, dk_in, dk_send, dk_recv, line).wait_recv()
        dk_own[...] += dk_in[line].astype(F32)

    each(z + 1, lines, dk_add)
    dk_ref[...] = dk_own[...].astype(BF16)

    def dq_add(i, total):
        dq_arrival(i).wait_recv()
        return total + dq_in[lax.div(far_peer(i), 2)].astype(F32)

    dq_total = lax.fori_loop(1, chips, dq_add, dq_total)
    dq_ref[...] = dq_total.T.astype(BF16)

    each(1, heads, lambda i: hop1(i).wait_send())
    each(1, ctxs, lambda i: hop2(i).wait_send())
    share_sent(qg, q_send, q_recv)
    share_sent(dog, do_send, do_recv)
    each(0, chips, lambda j: dq_near(j).wait_send())
    each(1, chips, lambda i: dq_away(i).wait_send())

    def stats_sent(i):
        stat(lse_st, l_send, l_recv, i).wait_send()
        stat(del_st, d_send, d_recv, i).wait_send()

    each(1, group, stats_sent)

    def lines_sent(line):
        to_line(kb, k_send, k_recv, line).wait_send()
        to_line(vb, v_send, v_recv, line).wait_send()

    each(z + 1, lines, lines_sent)

    def backs_sent(line):
        back(dv_out, dv_in, dv_send, dv_recv, line).wait_send()
        back(dk_out, dk_in, dk_send, dk_recv, line).wait_send()

    each(0, z, backs_sent)


def shards(heads, ctxs, group, queries, keys, values, teacher_rows, slots, spans):
    rows = queries.shape[0]
    trows = teacher_rows.shape[0]
    lines = ctxs // group
    chips = group // 2
    chunks = group * rows // CHUNK
    vm = pltpu.VMEM
    dma = pltpu.SemaphoreType.DMA
    scratch = [
        vm((1, trows), jnp.int32),
        vm((2, trows), jnp.int32),
        vm((heads, 64, DH), BF16),
        vm((heads, 64, DH), BF16),
        vm((ctxs, 32, DH), BF16),
        vm((ctxs, 32, DH), BF16),
        vm((group * rows, DH), BF16),
        vm((group * rows, DH), BF16),
        vm((lines, rows, DH), BF16),
        vm((lines, rows, DH), BF16),
        vm((lines, DH, rows), BF16),
        vm((lines, chunks, rows, CHUNK), F32),
        vm((lines, chunks, rows, CHUNK), BF16),
        vm((lines, chunks, rows, CHUNK), F32),
        vm((chunks, 1, CHUNK), F32),
        vm((group, chunks, 1, CHUNK), F32),
        vm((group, chunks, 1, CHUNK), F32),
        vm((chunks, 1, CHUNK), F32),
        vm((group, DH, rows), F32),
        vm((group, DH, rows), BF16),
        vm((chips, DH, rows), BF16),
        vm((chips, DH, rows), BF16),
        vm((chips, DH, rows), BF16),
        vm((lines, rows, DH), BF16),
        vm((lines, rows, DH), BF16),
        vm((rows, DH), F32),
        vm((lines, rows, DH), BF16),
        vm((lines, rows, DH), BF16),
        vm((rows, DH), F32),
        dma((5 + heads,)),
        dma((heads,)),
        dma((heads,)),
        dma((ctxs,)),
        dma((ctxs,)),
        dma((group,)),
        dma((group,)),
        dma((lines,)),
        dma((lines,)),
        dma((lines,)),
        dma((lines,)),
        dma((group,)),
        dma((group,)),
        dma((group,)),
        dma((group,)),
        dma((group,)),
        dma((group,)),
        dma((chips,)),
        dma((chips,)),
        dma((chips,)),
        dma((chips,)),
        dma((lines,)),
        dma((lines,)),
        dma((lines,)),
        dma((lines,)),
    ]
    out = jax.ShapeDtypeStruct((rows, DH), BF16)
    return pl.pallas_call(
        functools.partial(kernel, heads, ctxs, group),
        out_shape=(out, out, out),
        in_specs=[pl.BlockSpec(memory_space=pl.ANY)] * 6,
        out_specs=(pl.BlockSpec(memory_space=pltpu.VMEM),) * 3,
        scratch_shapes=scratch,
        compiler_params=pltpu.CompilerParams(
            collective_id=0, has_side_effects=True, vmem_limit_bytes=56 * 1024 * 1024
        ),
        name="attention_backward",
    )(queries, keys, values, teacher_rows, slots.reshape(1, trows), spans.T)


def solution(mesh):
    heads, ctxs = mesh.shape["head"], mesh.shape["ctx"]
    group = min(GROUP, ctxs // 2)
    return jax.shard_map(
        functools.partial(shards, heads, ctxs, group),
        mesh=mesh,
        in_specs=(
            P("ctx", "head"),
            P("ctx", "head"),
            P("ctx", "head"),
            P(("head", "ctx"), None),
            P(("head", "ctx")),
            P(("head", "ctx"), None),
        ),
        out_specs=(P("ctx", "head"), P("ctx", "head"), P("ctx", "head")),
        check_vma=False,
    )
```

time: 741 us -> 62.6 us (0.08); the launches traced: 731 us -> 62.4 us
  starting transfers between devices: 551 us -> 0 us
  waiting for transfers between devices: 99.1 us -> 0 us
  Pallas kernels: 0 us -> 58.8 us
  local copies, waits for them, and re-layouts: 53.4 us -> 3 us
  matrix products: 19.4 us -> 0 us
    ppermute x188 -> x0, starting transfers between devices: 522 us -> none  [the longest x124 434 us: from_behind(): return lax.ppermute(x, axis, pairs)]
    ppermute x188 -> x0, waiting for transfers between devices: 80.5 us -> none  [the longest x124 78.5 us: from_behind(): return lax.ppermute(x, axis, pairs)]
    pallas_call x0 -> x1, Pallas kernels: none -> 58.8 us  [shards(): pl.pallas_call(functools.partial(kernel, heads, ctxs, group), out_shape=(...]
    another operation x128 -> x0, local copies, waits for them, and re-layouts: 39.7 us -> none
    all_to_all x4 -> x0, starting transfers between devices: 29 us -> none  [the longest x1 11.4 us: shards(): lax.all_to_all(lax.all_to_all(bounds, 'head', split_axis=2, concat_axis=1...]
    dot_general x43 -> x0, matrix products: 19.4 us -> none  [the longest x12 7.7 us: block_scores(): jnp.einsum('qhd,khd->hqk', query_heads, key_heads, preferred_element_type...]
    all_to_all x4 -> x0, waiting for transfers between devices: 18.7 us -> none  [the longest x1 9.43 us: shards(): lax.all_to_all(lax.all_to_all(packed, 'head', split_axis=2, concat_axis=1...]
  transfers between devices with their start and end apart: 192 -> 0, of which waited for: 62 -> 0; matrix products, arithmetic and copies ran while one was open for 6% -> 0% of each run, Pallas kernels for 0% -> 0%
where the time goes in v1:
time: 62.6 us; the launch traced here: 62.4 us
  Pallas kernels  58.8 us (94%)
  local copies, waits for them, and re-layouts  3 us (5%)
  between operations  0.65 us (1%)
    pallas_call x1, Pallas kernels, shards(): pl.pallas_call(functools.partial(kernel, heads, ctxs, group), out_shape=(...  58.8 us
    unnamed x7, local copies, waits for them, and re-layouts  3 us

profile of v1, /device:TPU:37, one launch (start us, length us, event | category | flops | bytes accessed | tf_op | source)
XLA Modules:
  0.0 62.4 jit_solution(10504646877660805481)
XLA Ops:
  0.6 58.8 %attention_backward.1 = (bf16[256,128]{1,0:T(8,128)(2,1)}, bf16[256,128]{1,0:T(8,128)(2,1)}, bf16[256,128]{1,0:T(8,128)(2,1)}) custom-call(bf16[256,128]{1,0:T(8,128)(2,1)} %refs_0_.1, bf16[256,128]{1,0:T(8,128)(2,1)} %refs_1_.1, bf16[256,128]{1,0:T(8,128)(2,1)} %refs_2_.1, bf16[48,1024]{1,0:T(8,128)(2,1)} %refs_3_.1, s32[1,48]{1,0:T(1,128)} %bitcast.3, ...), custom_call_target="tpu_custom_call" | custom-call | tf_op jit(solution)/shard_map/attention_backward/pallas_call | solution.py:558
  59.4 0.0 copy-start.1
  59.4 1.5 %copy.12 = bf16[256,128]{1,0:T(8,128)(2,1)} copy(bf16[256,128]{1,0:T(8,128)(2,1)} %get-tuple-element.6) | data formatting | bytes 131072
  60.9 0.0 copy-done.1
  60.9 0.0 copy-start
  60.9 0.6 %copy.13 = bf16[256,128]{1,0:T(8,128)(2,1)} copy(bf16[256,128]{1,0:T(8,128)(2,1)S(1)} %copy-done.1) | data formatting | bytes 131072
  61.6 0.2 copy-done
  61.8 0.6 %copy.14 = bf16[256,128]{1,0:T(8,128)(2,1)} copy(bf16[256,128]{1,0:T(8,128)(2,1)S(1)} %copy-done) | data formatting | bytes 131072
Async XLA Ops:
  59.4 1.5 %copy-start.1 = (bf16[256,128]{1,0:T(8,128)(2,1)S(1)}, bf16[256,128]{1,0:T(8,128)(2,1)}, u32[]{:S(2)}) copy-start(bf16[256,128]{1,0:T(8,128)(2,1)} %get-tuple-element.7) | copy-start | bytes 196612
  60.9 0.9 %copy-start = (bf16[256,128]{1,0:T(8,128)(2,1)S(1)}, bf16[256,128]{1,0:T(8,128)(2,1)}, u32[]{:S(2)}) copy-start(bf16[256,128]{1,0:T(8,128)(2,1)} %get-tuple-element.8) | copy-start | bytes 196612
